TPU v7x, 32 devices: a whole 2x2x4 slice. The times are simulated.
32 devices in a mesh: row: 8 (over y, x, core), col: 4 (over z).
Axes of the slice: x: 2, y: 2, z: 4, core: 2. Of those that a mesh axis runs over, the one named last changes fastest.
Arguments:
- pair_rep: bfloat16 [512, 512, 128], P('row', 'col'), may hold values from -6 to 6
- token_mask: int32 [512], replicated, may hold values from 0 to 1, as said below
- in_gain: float32 [128], replicated, may hold values from 0.5 to 2
- in_bias: float32 [128], replicated, may hold values from -3 to 3
- left_weight: bfloat16 [128, 256], replicated, may hold values from -0.5 to 0.5
- right_weight: bfloat16 [128, 256], replicated, may hold values from -0.5 to 0.5
- gate_weight: bfloat16 [128, 128], replicated, may hold values from -0.5 to 0.5
- out_gain: float32 [128], replicated, may hold values from 0.5 to 2
- out_bias: float32 [128], replicated, may hold values from -3 to 3
- out_weight: bfloat16 [128, 128], replicated, may hold values from -0.5 to 0.5
Outputs:
- update: bfloat16 [512, 512, 128], P('row', 'col')
Inputs may be any that keep to these rules, and one draw needn't show every extreme that they name: `token_mask`: tokens lie in chains of 64 consecutive slots; in each chain a leading run of 32 to 64 slots is 1 and the rest is 0; the first chain is full and the second holds exactly 32 real tokens.
All inputs are finite; a program needn't handle non-finite values.
Results may differ from a plain program's by a relative error of at most 0.0053.
Values may be sent and summed in bfloat16 or wider, within the bound.
No kernel may reach another device: no remote copies, remote signals or barrier semaphores. Data moves between devices by JAX's collectives and lax.ppermute only.
A program may use at most 128 MiB of HBM per device.

v0:
```python
import jax
import jax.numpy as jnp
from jax import lax
from jax.sharding import PartitionSpec as P

EPS = 1e-05


def layer_norm(values, gain_vec, bias_vec, along):
    average = jnp.mean(values, axis=along, keepdims=True)
    centered = values - average
    variance = jnp.mean(centered * centered, axis=along, keepdims=True)
    return centered * lax.rsqrt(variance + EPS) * gain_vec + bias_vec


def shards(
    pair_rep,
    token_mask,
    in_gain,
    in_bias,
    left_weight,
    right_weight,
    gate_weight,
    out_gain,
    out_bias,
    out_weight,
):
    row_tok, col_tok, pair_width = pair_rep.shape
    hidden_width = out_weight.shape[0]
    row_count = lax.axis_size("row")
    col_count = lax.axis_size("col")
    validity = token_mask.astype(jnp.float32)
    row_valid = lax.dynamic_slice_in_dim(validity, lax.axis_index("row") * row_tok, row_tok)
    col_valid = lax.dynamic_slice_in_dim(validity, lax.axis_index("col") * col_tok, col_tok)
    pair_mask = row_valid[:, None] * col_valid[None, :]
    normed = layer_norm(pair_rep.astype(jnp.float32), in_gain, in_bias, 2).astype(jnp.bfloat16)
    gate_value = jax.nn.sigmoid(
        jnp.einsum("ijc,cd->ijd", normed, gate_weight, preferred_element_type=jnp.float32)
    )
    left_proj = jnp.einsum("ijc,cg->ijg", normed, left_weight, preferred_element_type=jnp.float32)
    right_proj = jnp.einsum("ijc,cg->ijg", normed, right_weight, preferred_element_type=jnp.float32)
    left_value = (
        jax.nn.sigmoid(left_proj[..., :hidden_width])
        * left_proj[..., hidden_width:]
        * pair_mask[..., None]
    ).astype(jnp.bfloat16)
    right_value = (
        jax.nn.sigmoid(right_proj[..., :hidden_width])
        * right_proj[..., hidden_width:]
        * pair_mask[..., None]
    ).astype(jnp.bfloat16)
    slab_width = col_tok // row_count
    stacked = left_value.reshape(row_tok, row_count, 1, slab_width, hidden_width)
    left_panel = lax.all_gather(stacked, "col", axis=2, tiled=True)
    left_panel = left_panel.reshape(row_tok, row_count * col_count * slab_width, hidden_width)
    right_routed = lax.all_to_all(
        lax.all_to_all(right_value, "row", split_axis=1, concat_axis=0, tiled=True),
        "col",
        split_axis=0,
        concat_axis=1,
        tiled=True,
    )
    product = jnp.einsum(
        "ikh,jkh->ijh",
        left_panel,
        lax.all_gather(right_routed, "row", axis=1, tiled=True),
        preferred_element_type=jnp.float32,
    )
    final_norm = layer_norm(product, out_gain, out_bias, 2).astype(jnp.bfloat16)
    update = gate_value * jnp.einsum(
        "ijh,hc->ijc", final_norm, out_weight, preferred_element_type=jnp.float32
    )
    return update.astype(jnp.bfloat16)


def solution(mesh):
    placed = (P("row", "col", None), P(), P(), P(), P(), P(), P(), P(), P(), P())
    return jax.shard_map(
        shards, mesh=mesh, in_specs=placed, out_specs=P("row", "col", None), check_vma=False
    )
```

profile of v0, /device:TPU:0, one launch (start us, length us, event | category | flops | bytes accessed | tf_op | source)
XLA Modules:
  0.0 336.8 jit_solution(4986473607429359956)
XLA Ops:
  6.6 0.8 convert_element_type.23
  7.4 0.1 dynamic_slice.6
  7.5 0.1 dynamic_slice.7
  7.6 2.2 convert_reduce_fusion
  9.8 3.6 %fusion.2 = f32[64,128]{1,0:T(8,128)S(1)} fusion(bf16[64,128,128]{2,1,0:T(8,128)(2,1)} %param.10, f32[64,128]{1,0:T(8,128)S(1)} %broadcast_multiply_fusion.2), kind=kLoop, calls=%fused_computation.4 | loop fusion | flops 4186112 | bytes 2162688 | tf_op jit(solution)/shard_map/reduce_sum | solution.py:12
  13.5 2.4 fusion.17
  15.8 2.4 fusion.19
  18.2 0.1 broadcast_multiply_fusion
  18.3 3.8 %fusion.7 = (bf16[64,128,128]{2,1,0:T(8,128)(2,1)}, bf16[64,128,128]{2,1,0:T(8,128)(2,1)}) fusion(f32[64,128,256]{2,1,0:T(8,128)S(1)} %fusion.19, f32[64,128]{1,0:T(8,128)S(1)} %broadcast_multiply_fusion, f32[64,128,256]{2,1,0:T(8,128)S(1)} %fusion.17), kind=kLoop, calls=%fused_computation.10 | loop fusion | flops 12582912 | bytes 21004288 | tf_op jit(solution)/shard_map/convert_element_type | solution.py:51
  22.1 2.9 copy.23
  25.1 31.6 %all_to_all.36 = bf16[64,128,128]{2,0,1:T(8,128)(2,1)S(1)} all-to-all(bf16[64,128,128]{2,0,1:T(8,128)(2,1)S(1)} %copy.23), channel_id=1, replica_groups=mesh['row'=8,'col'=4] {'row'}, dimensions={1} | all-to-all | bytes 4194304 | tf_op jit(solution)/shard_map/all_to_all | solution.py:57
  56.6 1.4 copy.25
  58.0 98.5 %all_to_all.37 = bf16[512,16,128]{2,1,0:T(8,128)(2,1)} all-to-all(bf16[512,16,128]{2,1,0:T(8,128)(2,1)S(1)} %bitcast.37), channel_id=1, replica_groups=mesh['row'=8,'col'=4] {'col'}, dimensions={0} | all-to-all | bytes 4194304 | tf_op jit(solution)/shard_map/all_to_all | solution.py:56
  156.5 5.1 %copy.26 = bf16[128,4,16,128]{0,2,1,3:T(8,128)(2,1)} copy(bf16[128,4,16,128]{3,2,0,1:T(8,128)(2,1)} %bitcast.38) | data formatting | bytes 4194304 | tf_op jit(solution)/shard_map/all_to_all | solution.py:56
  161.6 4.4 %fusion.23 = f32[64,128,128]{2,1,0:T(8,128)} fusion(bf16[64,128,128]{2,1,0:T(8,128)(2,1)S(1)} %copy-done.2, f32[128]{0:T(128)S(1)} %copy-done.6, f32[128]{0:T(128)S(1)} %copy-done.7, f32[64,128]{1,0:T(8,128)S(1)} %add_rsqrt_fusion.1, f32[64,128]{1,0:T(8,128)S(1)} %broadcast_multiply_fusion.2, bf16[128,128]{1,0:T(8,128)(2,1)S(1)} %copy-done.5), kind=kOutput, calls=%fused_computation.32 | convolution fusion | flops 274726912 | bytes 6390784 | tf_op jit(solution)/shard_map/ijc,cd->ijd/dot_general | solution.py:38
  166.0 53.7 %all-gather.5.cloned.1.call-done = bf16[64,8,4,16,128]{4,3,2,1,0:T(8,128)(2,1)} async-done(((bf16[64,8,1,16,128]{4,3,2,1,0:T(8,128)(2,1)}), bf16[64,8,4,16,128]{4,3,2,1,0:T(8,128)(2,1)}) %all-gather.5.cloned.1.call-update) | async-done | bytes 8388624 | tf_op jit(solution)/shard_map/all_gather | solution.py:54
  219.7 12.8 %copy.28 = bf16[64,512,128]{1,0,2:T(8,128)(2,1)} copy(bf16[64,512,128]{2,1,0:T(8,128)(2,1)} %bitcast.34) | data formatting | bytes 16777216 | tf_op jit(solution)/shard_map/reshape | solution.py:55
  232.5 79.1 %all-gather.3.cloned.1.call-done = bf16[128,512,128]{0,1,2:T(8,128)(2,1)} async-done(((bf16[128,64,128]{0,1,2:T(8,128)(2,1)}), bf16[128,512,128]{0,1,2:T(8,128)(2,1)}) %all-gather.3.cloned.1.call-update) | async-done | bytes 16777232 | tf_op jit(solution)/shard_map/all_gather | solution.py:66
  311.6 11.3 %bitcast_reduce_fusion = (f32[64,128]{1,0:T(8,128)S(1)}, f32[128,128,64]{1,2,0:T(8,128)S(1)}) fusion(bf16[64,512,128]{1,0,2:T(8,128)(2,1)} %copy.28, bf16[128,512,128]{0,1,2:T(8,128)(2,1)} %all-gather.3.cloned.1.call-done), kind=kOutput, calls=%fused_computation.23 | convolution fusion | flops 1074782208 | bytes 29392896 | tf_op jit(solution)/shard_map/ikh,jkh->ijh/dot_general | solution.py:63
  322.9 0.5 multiply_reduce_fusion
  323.4 0.1 copy-done.8
  323.6 0.8 add_convert_fusion
  324.3 1.3 copy-done.3
  325.6 4.3 %multiply_convert_fusion = bf16[64,128,128]{2,1,0:T(8,128)(2,1)} fusion(f32[64,128,128]{2,1,0:T(8,128)S(1)} %copy-done.3, bf16[64,128,128]{1,0,2:T(8,128)(2,1)S(1)} %add_convert_fusion, bf16[128,128]{1,0:T(8,128)(2,1)S(1)} %copy-done.10), kind=kOutput, calls=%fused_computation.24 | convolution fusion | flops 273678336 | bytes 8421376 | tf_op jit(solution)/shard_map/ijh,hc->ijc/dot_general | solution.py:70
  (28 shorter events, 0.2 us)
Async XLA Ops:
  6.5 6.9 %copy-start = (bf16[128,256]{1,0:T(8,128)(2,1)S(1)}, bf16[128,256]{1,0:T(8,128)(2,1)}, u32[]{:S(2)}) copy-start(bf16[128,256]{1,0:T(8,128)(2,1)} %param.14) | copy-start | bytes 196612
  6.5 6.9 %copy-start.2 = (bf16[64,128,128]{2,1,0:T(8,128)(2,1)S(1)}, bf16[64,128,128]{2,1,0:T(8,128)(2,1)}, u32[]{:S(2)}) copy-start(bf16[64,128,128]{2,1,0:T(8,128)(2,1)} %param.10) | copy-start | bytes 6291460
  6.5 6.9 %copy-start.7 = (f32[128]{0:T(128)S(1)}, f32[128]{0:T(128)}, u32[]{:S(2)}) copy-start(f32[128]{0:T(128)} %param.12) | copy-start | bytes 1540
  6.5 6.9 %copy-start.6 = (f32[128]{0:T(128)S(1)}, f32[128]{0:T(128)}, u32[]{:S(2)}) copy-start(f32[128]{0:T(128)} %param.13) | copy-start | bytes 1540
  6.5 213.1 %all-gather.5.cloned.1.call-start = ((), (), s32[]{:S(2)}) async-start(), calls=%async_computation.3 | async-start | bytes 10485760 | tf_op jit(solution)/shard_map/all_gather | solution.py:54
  13.4 2.4 copy-start.4
  22.1 289.5 %all-gather.3.cloned.1.call-start = ((), (), s32[]{:S(2)}) async-start(), calls=%async_computation.2 | async-start | bytes 18874368 | tf_op jit(solution)/shard_map/all_gather | solution.py:66
  156.5 5.1 %copy-start.5 = (bf16[128,128]{1,0:T(8,128)(2,1)S(1)}, bf16[128,128]{1,0:T(8,128)(2,1)}, u32[]{:S(2)}) copy-start(bf16[128,128]{1,0:T(8,128)(2,1)} %param.16) | copy-start | bytes 98308
  322.9 0.7 copy-start.8
  322.9 0.7 copy-start.9
  323.4 2.2 copy-start.3
  323.4 2.2 copy-start.10
  325.6 4.3 %copy-start.1 = (bf16[128,256]{1,0:T(8,128)(2,1)S(1)}, bf16[128,256]{1,0:T(8,128)(2,1)}, u32[]{:S(2)}) copy-start(bf16[128,256]{1,0:T(8,128)(2,1)} %param.14) | copy-start | bytes 196612
Sparse Core Ops, SparseCore 0:
  22.2 197.4 all-gather.4
  221.6 89.9 all-gather.2
where the time goes:
time: 337 us
  waiting for transfers between devices  133 us (39%)
  blocking collectives  130 us (39%)
  matrix products  24.7 us (7%)
  local copies, waits for them, and re-layouts  23.8 us (7%)
  between operations  13.6 us (4%)
  other arithmetic  11.7 us (3%)
    all_to_all x1, blocking collectives, shards(): lax.all_to_all(lax.all_to_all(right_value, 'row', split_axis=1, concat_ax...  98.5 us
    all_gather x1, waiting for transfers between devices, shards(): lax.all_gather(right_routed, 'row', axis=1, tiled=True)  79.1 us
    all_gather x1, waiting for transfers between devices, shards(): left_panel = lax.all_gather(stacked, 'col', axis=2, tiled=True)  53.7 us
    all_to_all x1, blocking collectives, shards(): lax.all_to_all(right_value, 'row', split_axis=1, concat_axis=0, tiled=True)  31.6 us
    reshape x1, local copies, waits for them, and re-layouts, shards(): left_panel.reshape(row_tok, row_count * col_count * slab_width, hidden_wi...  12.8 us
    dot_general x1, matrix products, shards(): jnp.einsum('ikh,jkh->ijh', left_panel, lax.all_gather(right_routed, 'row'...  11.3 us
  transfers between devices with their start and end apart: 2, of which 2 were waited for; matrix products, arithmetic and copies ran while one was open for 8% of the time, Pallas kernels for 0%

commit v1 on v0

v1 whole, which is shorter than its diff:
```python
import functools

import jax
import jax.numpy as jnp
from jax import lax
from jax.experimental import pallas as pl
from jax.experimental.pallas import tpu as pltpu
from jax.sharding import PartitionSpec as P

EPS = 1e-05
F32 = jnp.float32
BF16 = jnp.bfloat16
ROW_TILE = 16
PARAMS = pltpu.CompilerParams(vmem_limit_bytes=56 * 2**20)


def whole(array):
    return pl.BlockSpec(array.shape, lambda *_: (0,) * array.ndim)


def project(normed, mask_ref, left_ref, right_ref, out_ref, low, width):
    rows, cols, pair_width = normed.shape
    hidden = left_ref.shape[1] // 2
    half = jnp.asarray(0.5, BF16)
    left = left_ref[...].T * half
    right = right_ref[...].T * half
    weight = jnp.concatenate(
        [
            left[low : low + width],
            right[low : low + width],
            left[hidden + low : hidden + low + width],
            right[hidden + low : hidden + low + width],
        ],
        0,
    )
    pieces = []
    for i in range(0, rows, 2):
        two = normed[i : i + 2].reshape(2 * cols, pair_width)
        proj = lax.dot_general(
            weight, two, (((1,), (1,)), ((), ())), preferred_element_type=F32
        )
        value = ((jnp.tanh(proj[: 2 * width]) + 1.0) * proj[2 * width :]).astype(BF16)
        pieces += [value[:, :cols], value[:, cols:]]
    value = jnp.swapaxes(jnp.stack(pieces, 0), 0, 1) * mask_ref[...][None]
    dests, _, share = out_ref.shape[:3]
    for side in range(2):
        part = value[side * width : (side + 1) * width]
        out_ref[:, side] = part.reshape(dests, share, rows, cols)


def first_kernel(
    pair_ref, mask_ref, left_ref, right_ref, gain_ref, bias_ref, normed_ref, out_ref, *, low, width
):
    value = pair_ref[...].astype(F32)
    average = jnp.mean(value, axis=-1, keepdims=True)
    centered = value - average
    variance = jnp.mean(centered * centered, axis=-1, keepdims=True)
    normed = (centered * lax.rsqrt(variance + EPS) * gain_ref[...] + bias_ref[...]).astype(BF16)
    normed_ref[...] = normed
    project(normed, mask_ref, left_ref, right_ref, out_ref, low, width)


def later_kernel(normed_ref, mask_ref, left_ref, right_ref, out_ref, *, low, width):
    project(normed_ref[...], mask_ref, left_ref, right_ref, out_ref, low, width)


def gate_kernel(normed_ref, weight_ref, gate_ref):
    rows, cols, pair_width = normed_ref.shape
    half = jnp.asarray(0.5, BF16)
    proj = jnp.dot(
        normed_ref[...].reshape(rows * cols, pair_width),
        weight_ref[...] * half,
        preferred_element_type=F32,
    )
    gate_ref[...] = (0.5 * jnp.tanh(proj) + 0.5).reshape(gate_ref.shape)


def panel(ref, side, start, count):
    parts = []
    for z in range(ref.shape[1]):
        block = ref[pl.ds(start, count), z, side, 0]
        parts.append(block.reshape(count * block.shape[1], block.shape[2]))
    return jnp.concatenate(parts, 1)


def times(left, right):
    return lax.dot_general(left, right, (((1,), (1,)), ((), ())), preferred_element_type=F32)


def far_kernel(half_ref, edges_ref, far_ref):
    devices = edges_ref.shape[0]
    left = panel(edges_ref, 0, 0, devices)
    right = panel(edges_ref, 1, (1 - half_ref[0]) * (devices // 2), devices // 2)
    far_ref[0] = times(left, right).astype(BF16)


def near_kernel(half_ref, edges_ref, far_ref, out_ref):
    devices, groups, _, rows, cols = out_ref.shape
    left = panel(edges_ref, 0, 0, devices)
    right = panel(edges_ref, 1, half_ref[0] * (devices // 2), devices // 2)
    total = (times(left, right) + far_ref[0].astype(F32)).astype(BF16)
    for z in range(groups):
        out_ref[:, z, 0] = total[:, z * cols : (z + 1) * cols].reshape(devices, rows, cols)


def last_kernel(*refs):
    gate_ref, gain_ref, bias_ref, weight_ref = refs[:4]
    out_ref = refs[-1]
    rows, cols = gate_ref.shape[:2]
    parts = []
    for ref in refs[4:-1]:
        parts.append(ref[...].reshape(ref.shape[0] * ref.shape[1], rows, cols))
    value = jnp.swapaxes(jnp.concatenate(parts, 0), 0, 1)
    weight = weight_ref[...]
    for i in range(rows):
        product = value[i].astype(F32)
        average = jnp.mean(product, axis=0, keepdims=True)
        centered = product - average
        variance = jnp.mean(centered * centered, axis=0, keepdims=True)
        normed = centered * lax.rsqrt(variance + EPS) * gain_ref[...] + bias_ref[...]
        update = lax.dot_general(
            normed.astype(BF16), weight, (((0,), (0,)), ((), ())), preferred_element_type=F32
        )
        out_ref[i] = (gate_ref[i] * update).astype(BF16)


def shards(
    pair_rep,
    token_mask,
    in_gain,
    in_bias,
    left_weight,
    right_weight,
    gate_weight,
    out_gain,
    out_bias,
    out_weight,
):
    rows, cols, pair_width = pair_rep.shape
    hidden = out_weight.shape[0]
    row_count = lax.axis_size("row")
    col_count = lax.axis_size("col")
    group_cols = col_count // 2
    half = lax.axis_index("col") // group_cols
    members = row_count * group_cols
    share = hidden // members
    chunks = 2 if share % 2 == 0 else 1
    share //= chunks
    width = hidden // chunks
    axes = ("row", "col")
    groups = [
        [r * col_count + h * group_cols + z for r in range(row_count) for z in range(group_cols)]
        for h in range(2)
    ]
    across = [(c, (c + group_cols) % col_count) for c in range(col_count)]
    half_arg = jnp.reshape(half, (1,)).astype(jnp.int32)

    row_valid = lax.dynamic_slice_in_dim(token_mask, lax.axis_index("row") * rows, rows)
    col_valid = lax.dynamic_slice_in_dim(token_mask, lax.axis_index("col") * cols, cols)
    mask = (row_valid[:, None] * col_valid[None, :]).astype(BF16)

    tile = min(ROW_TILE, rows)
    steps = rows // tile
    by_row = lambda *tail: pl.BlockSpec((tile,) + tail, lambda i: (i,) + (0,) * len(tail))
    edge_shape = jax.ShapeDtypeStruct((members, 2, share, rows, cols), BF16)
    edge_spec = pl.BlockSpec((members, 2, share, tile, cols), lambda i: (0, 0, 0, i, 0))
    edges = []
    normed, first = pl.pallas_call(
        functools.partial(first_kernel, low=0, width=width),
        grid=(steps,),
        in_specs=[
            by_row(cols, pair_width),
            by_row(cols),
            whole(left_weight),
            whole(right_weight),
            whole(in_gain[None]),
            whole(in_bias[None]),
        ],
        out_specs=[by_row(cols, pair_width), edge_spec],
        out_shape=[jax.ShapeDtypeStruct(pair_rep.shape, BF16), edge_shape],
        compiler_params=PARAMS,
        name="norm_project",
    )(pair_rep, mask, left_weight, right_weight, in_gain[None], in_bias[None])
    edges.append(first)
    for t in range(1, chunks):
        edges.append(
            pl.pallas_call(
                functools.partial(later_kernel, low=t * width, width=width),
                grid=(steps,),
                in_specs=[
                    by_row(cols, pair_width),
                    by_row(cols),
                    whole(left_weight),
                    whole(right_weight),
                ],
                out_specs=edge_spec,
                out_shape=edge_shape,
                compiler_params=PARAMS,
                cost_estimate=pl.CostEstimate(
                    flops=4 * rows * cols * pair_width * width * 2,
                    bytes_accessed=3 * rows * cols * pair_width * 2,
                    transcendentals=rows * cols * width * 2,
                ),
                name="project",
            )(normed, mask, left_weight, right_weight)
        )
    gate = pl.pallas_call(
        gate_kernel,
        grid=(steps,),
        in_specs=[by_row(cols, pair_width), whole(gate_weight)],
        out_specs=by_row(cols, pair_width),
        out_shape=jax.ShapeDtypeStruct(pair_rep.shape, F32),
        compiler_params=PARAMS,
        cost_estimate=pl.CostEstimate(
            flops=2 * rows * cols * pair_width * pair_width,
            bytes_accessed=rows * cols * pair_width * 6,
            transcendentals=rows * cols * pair_width,
        ),
        name="gate",
    )(normed, gate_weight)

    def exchange(value):
        return lax.all_to_all(value, axes, 0, 0, axis_index_groups=groups, tiled=True)

    tokens = row_count * rows
    near_tokens = group_cols * cols
    one_h = pl.BlockSpec(
        (row_count, group_cols, 2, 1, rows, cols), lambda h, _: (0, 0, 0, h, 0, 0)
    )
    far_spec = pl.BlockSpec((1, tokens, near_tokens), lambda h, _: (h, 0, 0))
    product_cost = pl.CostEstimate(
        flops=2 * share * tokens * near_tokens * near_tokens,
        bytes_accessed=share * tokens * near_tokens * 6,
        transcendentals=0,
    )
    arrived = []
    fars = []
    for t in range(chunks):
        here = exchange(edges[t]).reshape(row_count, group_cols, 2, share, rows, cols)
        arrived.append(here)
        far = pl.pallas_call(
            far_kernel,
            grid_spec=pltpu.PrefetchScalarGridSpec(
                num_scalar_prefetch=1, grid=(share,), in_specs=[one_h], out_specs=far_spec
            ),
            out_shape=jax.ShapeDtypeStruct((share, tokens, near_tokens), BF16),
            compiler_params=PARAMS,
            cost_estimate=product_cost,
            name="far_product",
        )(half_arg, here)
        fars.append(lax.ppermute(far, "col", across))
    back = []
    for t in range(chunks):
        total = pl.pallas_call(
            near_kernel,
            grid_spec=pltpu.PrefetchScalarGridSpec(
                num_scalar_prefetch=1,
                grid=(share,),
                in_specs=[one_h, far_spec],
                out_specs=pl.BlockSpec(
                    (row_count, group_cols, 1, rows, cols), lambda h, _: (0, 0, h, 0, 0)
                ),
            ),
            out_shape=jax.ShapeDtypeStruct((row_count, group_cols, share, rows, cols), BF16),
            compiler_params=PARAMS,
            cost_estimate=product_cost,
            name="near_product",
        )(half_arg, arrived[t], fars[t])
        back.append(exchange(total.reshape(members, share, rows, cols)))

    gain_cols = jnp.broadcast_to(out_gain[:, None], (hidden, cols))
    bias_cols = jnp.broadcast_to(out_bias[:, None], (hidden, cols))
    piece = pl.BlockSpec((members, share, tile, cols), lambda i: (0, 0, i, 0))
    return pl.pallas_call(
        last_kernel,
        grid=(steps,),
        in_specs=[
            by_row(cols, pair_width),
            whole(gain_cols),
            whole(bias_cols),
            whole(out_weight),
        ]
        + [piece] * chunks,
        out_specs=by_row(cols, pair_width),
        out_shape=jax.ShapeDtypeStruct(pair_rep.shape, BF16),
        compiler_params=PARAMS,
        name="norm_out",
    )(gate, gain_cols, bias_cols, out_weight, *back)


def solution(mesh):
    placed = (P("row", "col", None), P(), P(), P(), P(), P(), P(), P(), P(), P())
    return jax.shard_map(
        shards, mesh=mesh, in_specs=placed, out_specs=P("row", "col", None), check_vma=False
    )
```

time: 337 us -> 198 us (0.59)
  blocking collectives: 130 us -> 0 us
  Pallas kernels: 0 us -> 39.7 us
  starting transfers between devices: 0.08 us -> 25 us
  matrix products: 24.7 us -> 0 us
  local copies, waits for them, and re-layouts: 23.8 us -> 6.37 us
  between operations: 13.6 us -> 0.09 us
  other arithmetic: 11.7 us -> 0.68 us
  waiting for transfers between devices: 133 us -> 126 us
    all_gather x2 -> x0, waiting for transfers between devices: 133 us -> none  [the longest x1 79.1 us: shards(): lax.all_gather(right_routed, 'row', axis=1, tiled=True)]
    all_to_all x2 -> x0, blocking collectives: 130 us -> none  [the longest x1 98.5 us: shards(): lax.all_to_all(lax.all_to_all(right_value, 'row', split_axis=1, concat_ax...]
    ppermute x0 -> x2, waiting for transfers between devices: none -> 92.9 us  [shards(): fars.append(lax.ppermute(far, 'col', across))]
    pallas_call x0 -> x8, Pallas kernels: none -> 39.7 us  [the longest x2 8.48 us: shards(): pl.pallas_call(near_kernel, grid_spec=pltpu.PrefetchScalarGridSpec(num_sc...]
    all_to_all x0 -> x4, waiting for transfers between devices: none -> 32.8 us  [exchange(): lax.all_to_all(value, axes, 0, 0, axis_index_groups=groups, tiled=True)]
    dot_general x5 -> x0, matrix products: 24.7 us -> none  [the longest x1 11.3 us: shards(): jnp.einsum('ikh,jkh->ijh', left_panel, lax.all_gather(right_routed, 'row'...]
    all_to_all x0 -> x4, starting transfers between devices: none -> 19.1 us  [exchange(): lax.all_to_all(value, axes, 0, 0, axis_index_groups=groups, tiled=True)]
    reshape x1 -> x0, local copies, waits for them, and re-layouts: 12.8 us -> none  [shards(): left_panel.reshape(row_tok, row_count * col_count * slab_width, hidden_wi...]
  transfers between devices with their start and end apart: 2 -> 6, of which waited for: 2 -> 4; matrix products, arithmetic and copies ran while one was open for 8% -> 0% of each run, Pallas kernels for 0% -> 13%
where the time goes in v1:
time: 198 us
  waiting for transfers between devices  126 us (64%)
  Pallas kernels  39.7 us (20%)
  starting transfers between devices  25 us (13%)
  local copies, waits for them, and re-layouts  6.37 us (3%)
    ppermute x2, waiting for transfers between devices, shards(): fars.append(lax.ppermute(far, 'col', across))  92.9 us
    all_to_all x4, waiting for transfers between devices, exchange(): lax.all_to_all(value, axes, 0, 0, axis_index_groups=groups, tiled=True)  32.8 us
    all_to_all x4, starting transfers between devices, exchange(): lax.all_to_all(value, axes, 0, 0, axis_index_groups=groups, tiled=True)  19.1 us
    pallas_call x2, Pallas kernels, shards(): pl.pallas_call(near_kernel, grid_spec=pltpu.PrefetchScalarGridSpec(num_sc...  8.48 us
    pallas_call x2, Pallas kernels, shards(): pl.pallas_call(far_kernel, grid_spec=pltpu.PrefetchScalarGridSpec(num_sca...  8.18 us
    pallas_call x1, Pallas kernels, shards(): pl.pallas_call(functools.partial(first_kernel, low=0, width=width), grid=...  6.99 us
    pallas_call x1, Pallas kernels, shards(): pl.pallas_call(last_kernel, grid=(steps,), in_specs=[by_row(cols, pair_wi...  6.26 us
    ppermute x2, starting transfers between devices, shards(): fars.append(lax.ppermute(far, 'col', across))  5.87 us
  transfers between devices with their start and end apart: 6, of which 4 were waited for; matrix products, arithmetic and copies ran while one was open for 0% of the time, Pallas kernels for 13%

profile of v1, /device:TPU:0, one launch (start us, length us, event | category | flops | bytes accessed | tf_op | source)
XLA Modules:
  0.0 197.5 jit_solution(17545690282871897069)
XLA Ops:
  0.0 0.8 dynamic_slice.7
  0.8 0.8 dynamic_slice.6
  2.2 7.0 %norm_project.1 = (bf16[64,128,128]{2,1,0:T(8,128)(2,1)}, bf16[16,2,4,64,128]{4,3,2,1,0:T(8,128)(2,1)}) custom-call(bf16[64,128,128]{2,1,0:T(8,128)(2,1)} %pair_ref.1, bf16[64,128]{1,0:T(8,128)(2,1)} %multiply_convert_fusion.mask_ref, bf16[128,256]{1,0:T(8,128)(2,1)} %left_ref.3, bf16[128,256]{1,0:T(8,128)(2,1)} %right_ref.3, f32[1,128]{1,0:T(1,128)} %bitcast.13, ...), custom_call_target="tpu_custom_call" | custom-call | tf_op jit(solution)/shard_map/norm_project/pallas_call | solution.py:168
  9.2 6.3 %all-to-all-start = ((bf16[16,2,4,64,128]{4,3,2,1,0:T(8,128)(2,1)}), bf16[16,2,4,64,128]{4,3,2,1,0:T(8,128)(2,1)S(1)}, u32[]{:S(2)}, u32[]{:S(2)}) async-start(bf16[16,2,4,64,128]{4,3,2,1,0:T(8,128)(2,1)} %get-tuple-element.8), calls=%async_computation | async-start | bytes 4194304 | tf_op jit(solution)/shard_map/all_to_all | solution.py:223
  15.5 5.1 %project.1 = bf16[16,2,4,64,128]{4,3,2,1,0:T(8,128)(2,1)} custom-call(bf16[64,128,128]{2,1,0:T(8,128)(2,1)} %get-tuple-element.7.normed_ref, bf16[64,128]{1,0:T(8,128)(2,1)} %multiply_convert_fusion.mask_ref, bf16[128,256]{1,0:T(8,128)(2,1)} %left_ref.3, bf16[128,256]{1,0:T(8,128)(2,1)} %right_ref.3), custom_call_target="tpu_custom_call" | custom-call | flops 536870912 | bytes 6291456 | tf_op jit(solution)/shard_map/project/pallas_call | solution.py:187
  20.5 22.6 %all-to-all-done = bf16[16,2,4,64,128]{4,3,2,1,0:T(8,128)(2,1)S(1)} async-done(((bf16[16,2,4,64,128]{4,3,2,1,0:T(8,128)(2,1)}), bf16[16,2,4,64,128]{4,3,2,1,0:T(8,128)(2,1)S(1)}, u32[]{:S(2)}, u32[]{:S(2)}) %all-to-all-start) | async-done | bytes 2097184 | tf_op jit(solution)/shard_map/all_to_all | solution.py:223
  43.1 1.3 copy-done.1
  44.4 4.4 %all-to-all-start.2 = ((bf16[16,2,4,64,128]{4,3,2,1,0:T(8,128)(2,1)}), bf16[16,2,4,64,128]{4,3,2,1,0:T(8,128)(2,1)S(1)}, u32[]{:S(2)}, u32[]{:S(2)}) async-start(bf16[16,2,4,64,128]{4,3,2,1,0:T(8,128)(2,1)} %project.1), calls=%async_computation.2 | async-start | bytes 4194304 | tf_op jit(solution)/shard_map/all_to_all | solution.py:223
  48.8 4.1 %far_product.2 = bf16[4,512,256]{2,1,0:T(8,128)(2,1)} custom-call(s32[1]{0:T(128)} %bitcast.2.half_ref, bf16[8,2,2,4,64,128]{5,4,3,2,1,0:T(8,128)(2,1)} %bitcast.9), custom_call_target="tpu_custom_call" | custom-call | flops 268435456 | bytes 3145728 | tf_op jit(solution)/shard_map/far_product/pallas_call | solution.py:241
  52.9 2.6 %collective-permute-start = (bf16[4,512,256]{2,1,0:T(8,128)(2,1)}, bf16[4,512,256]{2,1,0:T(8,128)(2,1)S(1)}, u32[]{:S(2)}, u32[]{:S(2)}) collective-permute-start(bf16[4,512,256]{2,1,0:T(8,128)(2,1)} %far_product.2), channel_id=1, source_target_pairs={{0,2},{1,3},{2,0},{3,1},{4,6},{5,7},{6,4},{7,5},{8,10},{9,11},{10,... | collective-permute-start | bytes 3145736 | tf_op jit(solution)/shard_map/ppermute | solution.py:251
  55.5 46.5 %collective-permute-done.far_ref = bf16[4,512,256]{2,1,0:T(8,128)(2,1)S(1)} collective-permute-done((bf16[4,512,256]{2,1,0:T(8,128)(2,1)}, bf16[4,512,256]{2,1,0:T(8,128)(2,1)S(1)}, u32[]{:S(2)}, u32[]{:S(2)}) %collective-permute-start) | collective-permute-done | bytes 1048608 | tf_op jit(solution)/shard_map/ppermute | solution.py:251
  102.0 1.0 copy-done.5
  103.0 4.2 %near_product.2 = bf16[8,2,4,64,128]{4,3,2,1,0:T(8,128)(2,1)} custom-call(s32[1]{0:T(128)} %bitcast.2.half_ref, bf16[8,2,2,4,64,128]{5,4,3,2,1,0:T(8,128)(2,1)} %bitcast.10, bf16[4,512,256]{2,1,0:T(8,128)(2,1)} %copy-done.5), custom_call_target="tpu_custom_call" | custom-call | flops 268435456 | bytes 3145728 | tf_op jit(solution)/shard_map/near_product/pallas_call | solution.py:254
  107.3 4.2 %all-to-all-start.1 = ((bf16[16,4,64,128]{3,2,1,0:T(8,128)(2,1)}), bf16[16,4,64,128]{3,2,1,0:T(8,128)(2,1)S(1)}, u32[]{:S(2)}, u32[]{:S(2)}) async-start(bf16[16,4,64,128]{3,2,1,0:T(8,128)(2,1)} %bitcast.11), calls=%async_computation.1 | async-start | bytes 2097152 | tf_op jit(solution)/shard_map/all_to_all | solution.py:223
  111.4 4.1 %far_product.3 = bf16[4,512,256]{2,1,0:T(8,128)(2,1)} custom-call(s32[1]{0:T(128)} %bitcast.2.half_ref, bf16[8,2,2,4,64,128]{5,4,3,2,1,0:T(8,128)(2,1)} %bitcast.7), custom_call_target="tpu_custom_call" | custom-call | flops 268435456 | bytes 3145728 | tf_op jit(solution)/shard_map/far_product/pallas_call | solution.py:241
  115.5 3.2 %collective-permute-start.1 = (bf16[4,512,256]{2,1,0:T(8,128)(2,1)}, bf16[4,512,256]{2,1,0:T(8,128)(2,1)S(1)}, u32[]{:S(2)}, u32[]{:S(2)}) collective-permute-start(bf16[4,512,256]{2,1,0:T(8,128)(2,1)} %far_product.3), channel_id=1, source_target_pairs={{0,2},{1,3},{2,0},{3,1},{4,6},{5,7},{6,4},{7,5},{8,10},{9,11},{10,... | collective-permute-start | bytes 3145736 | tf_op jit(solution)/shard_map/ppermute | solution.py:251
  118.8 46.5 %collective-permute-done.1.far_ref = bf16[4,512,256]{2,1,0:T(8,128)(2,1)S(1)} collective-permute-done((bf16[4,512,256]{2,1,0:T(8,128)(2,1)}, bf16[4,512,256]{2,1,0:T(8,128)(2,1)S(1)}, u32[]{:S(2)}, u32[]{:S(2)}) %collective-permute-start.1) | collective-permute-done | bytes 1048608 | tf_op jit(solution)/shard_map/ppermute | solution.py:251
  165.2 1.0 copy-done.4
  166.2 4.3 %near_product.3 = bf16[8,2,4,64,128]{4,3,2,1,0:T(8,128)(2,1)} custom-call(s32[1]{0:T(128)} %bitcast.2.half_ref, bf16[8,2,2,4,64,128]{5,4,3,2,1,0:T(8,128)(2,1)} %bitcast.8, bf16[4,512,256]{2,1,0:T(8,128)(2,1)} %copy-done.4), custom_call_target="tpu_custom_call" | custom-call | flops 268435456 | bytes 3145728 | tf_op jit(solution)/shard_map/near_product/pallas_call | solution.py:254
  170.5 4.2 %all-to-all-start.3 = ((bf16[16,4,64,128]{3,2,1,0:T(8,128)(2,1)}), bf16[16,4,64,128]{3,2,1,0:T(8,128)(2,1)S(1)}, u32[]{:S(2)}, u32[]{:S(2)}) async-start(bf16[16,4,64,128]{3,2,1,0:T(8,128)(2,1)} %bitcast.12), calls=%async_computation.3 | async-start | bytes 2097152 | tf_op jit(solution)/shard_map/all_to_all | solution.py:223
  174.7 4.7 %gate.1.refs_0_ = f32[64,128,128]{2,1,0:T(8,128)} custom-call(bf16[64,128,128]{2,1,0:T(8,128)(2,1)} %get-tuple-element.7.normed_ref, bf16[128,128]{1,0:T(8,128)(2,1)} %weight_ref.1), custom_call_target="tpu_custom_call" | custom-call | flops 268435456 | bytes 6291456 | tf_op jit(solution)/shard_map/gate/pallas_call | solution.py:207
  179.4 10.3 %all-to-all-done.3.refs_5_ = bf16[16,4,64,128]{3,2,1,0:T(8,128)(2,1)S(1)} async-done(((bf16[16,4,64,128]{3,2,1,0:T(8,128)(2,1)}), bf16[16,4,64,128]{3,2,1,0:T(8,128)(2,1)S(1)}, u32[]{:S(2)}, u32[]{:S(2)}) %all-to-all-start.3) | async-done | bytes 1048608 | tf_op jit(solution)/shard_map/all_to_all | solution.py:223
  189.7 0.8 broadcast_in_dim.10.refs_1_
  191.2 6.3 %norm_out.1 = bf16[64,128,128]{2,1,0:T(8,128)(2,1)} custom-call(f32[64,128,128]{2,1,0:T(8,128)} %gate.1.refs_0_, f32[128,128]{1,0:T(8,128)} %broadcast_in_dim.10.refs_1_, f32[128,128]{1,0:T(8,128)} %broadcast_in_dim.11.refs_2_, bf16[128,128]{1,0:T(8,128)(2,1)} %refs_3_.1, bf16[16,4,64,128]{3,2,1,0:T(8,128)(2,1)} %copy-done.2, bf16[16,4,64,128]{3,2,1,0:T(8,128)(2,1)} %copy-done.3), custom_call_target="tpu_custom_call" | custom-call | tf_op jit(solution)/shard_map/norm_out/pallas_call | solution.py:274
  (17 shorter events, 1.4 us)
Async XLA Ops:
  9.2 33.9 %all-to-all-start = ((bf16[16,2,4,64,128]{4,3,2,1,0:T(8,128)(2,1)}), bf16[16,2,4,64,128]{4,3,2,1,0:T(8,128)(2,1)S(1)}, u32[]{:S(2)}, u32[]{:S(2)}) async-start(bf16[16,2,4,64,128]{4,3,2,1,0:T(8,128)(2,1)} %get-tuple-element.8), calls=%async_computation | async-start | bytes 4194304 | tf_op jit(solution)/shard_map/all_to_all | solution.py:223
  43.1 1.3 copy-start.1
  44.4 62.8 %all-to-all-start.2 = ((bf16[16,2,4,64,128]{4,3,2,1,0:T(8,128)(2,1)}), bf16[16,2,4,64,128]{4,3,2,1,0:T(8,128)(2,1)S(1)}, u32[]{:S(2)}, u32[]{:S(2)}) async-start(bf16[16,2,4,64,128]{4,3,2,1,0:T(8,128)(2,1)} %project.1), calls=%async_computation.2 | async-start | bytes 4194304 | tf_op jit(solution)/shard_map/all_to_all | solution.py:223
  52.9 49.1 %collective-permute-start = (bf16[4,512,256]{2,1,0:T(8,128)(2,1)}, bf16[4,512,256]{2,1,0:T(8,128)(2,1)S(1)}, u32[]{:S(2)}, u32[]{:S(2)}) collective-permute-start(bf16[4,512,256]{2,1,0:T(8,128)(2,1)} %far_product.2), channel_id=1, source_target_pairs={{0,2},{1,3},{2,0},{3,1},{4,6},{5,7},{6,4},{7,5},{8,10},{9,11},{10,... | collective-permute-start | bytes 3145736 | tf_op jit(solution)/shard_map/ppermute | solution.py:251
  102.0 1.0 copy-start.5
  107.3 4.2 %copy-start = (bf16[16,2,4,64,128]{4,3,2,1,0:T(8,128)(2,1)}, bf16[16,2,4,64,128]{4,3,2,1,0:T(8,128)(2,1)S(1)}, u32[]{:S(2)}) copy-start(bf16[16,2,4,64,128]{4,3,2,1,0:T(8,128)(2,1)S(1)} %all-to-all-done.2) | copy-start | bytes 6291460
  107.3 63.2 %all-to-all-start.1 = ((bf16[16,4,64,128]{3,2,1,0:T(8,128)(2,1)}), bf16[16,4,64,128]{3,2,1,0:T(8,128)(2,1)S(1)}, u32[]{:S(2)}, u32[]{:S(2)}) async-start(bf16[16,4,64,128]{3,2,1,0:T(8,128)(2,1)} %bitcast.11), calls=%async_computation.1 | async-start | bytes 2097152 | tf_op jit(solution)/shard_map/all_to_all | solution.py:223
  115.5 49.7 %collective-permute-start.1 = (bf16[4,512,256]{2,1,0:T(8,128)(2,1)}, bf16[4,512,256]{2,1,0:T(8,128)(2,1)S(1)}, u32[]{:S(2)}, u32[]{:S(2)}) collective-permute-start(bf16[4,512,256]{2,1,0:T(8,128)(2,1)} %far_product.3), channel_id=1, source_target_pairs={{0,2},{1,3},{2,0},{3,1},{4,6},{5,7},{6,4},{7,5},{8,10},{9,11},{10,... | collective-permute-start | bytes 3145736 | tf_op jit(solution)/shard_map/ppermute | solution.py:251
  165.2 1.0 copy-start.4
  170.5 9.0 %copy-start.2 = (bf16[16,4,64,128]{3,2,1,0:T(8,128)(2,1)}, bf16[16,4,64,128]{3,2,1,0:T(8,128)(2,1)S(1)}, u32[]{:S(2)}) copy-start(bf16[16,4,64,128]{3,2,1,0:T(8,128)(2,1)S(1)} %all-to-all-done.1.refs_4_) | copy-start | bytes 3145732
  170.5 19.2 %all-to-all-start.3 = ((bf16[16,4,64,128]{3,2,1,0:T(8,128)(2,1)}), bf16[16,4,64,128]{3,2,1,0:T(8,128)(2,1)S(1)}, u32[]{:S(2)}, u32[]{:S(2)}) async-start(bf16[16,4,64,128]{3,2,1,0:T(8,128)(2,1)} %bitcast.12), calls=%async_computation.3 | async-start | bytes 2097152 | tf_op jit(solution)/shard_map/all_to_all | solution.py:223
  174.7 15.0 %copy-start.6 = (f32[128]{0:T(128)S(1)}, f32[128]{0:T(128)}, u32[]{:S(2)}) copy-start(f32[128]{0:T(128)} %param.17) | copy-start | bytes 1540
  174.7 15.8 %copy-start.7 = (f32[128]{0:T(128)S(1)}, f32[128]{0:T(128)}, u32[]{:S(2)}) copy-start(f32[128]{0:T(128)} %param.18) | copy-start | bytes 1540
  189.7 1.5 copy-start.3

commit v2 on v1

v2 whole, which is shorter than its diff:
```python
import functools

import jax
import jax.numpy as jnp
from jax import lax
from jax.experimental import pallas as pl
from jax.experimental.pallas import tpu as pltpu
from jax.sharding import PartitionSpec as P

EPS = 1e-05
F32 = jnp.float32
BF16 = jnp.bfloat16
ROW_TILE = 16
CHUNKS = 2
PARAMS = pltpu.CompilerParams(vmem_limit_bytes=56 * 2**20)
NT = (((1,), (1,)), ((), ()))
SIZES = ((12, 0), (13, 2), (14, 4), (16, 16))


def whole(array):
    return pl.BlockSpec(array.shape, lambda *_: (0,) * array.ndim)


def dot(left, right, dims=(((1,), (0,)), ((), ()))):
    return lax.dot_general(left, right, dims, preferred_element_type=F32)


def project(normed, step, tokens_ref, cols_ref, left_ref, right_ref, out_ref, low, width):
    rows, cols, pair_width = normed.shape
    hidden = left_ref.shape[1] // 2
    half = jnp.asarray(0.5, BF16)
    left = left_ref[...].T * half
    right = right_ref[...].T * half
    weight = jnp.concatenate(
        [
            left[low : low + width],
            right[low : low + width],
            left[hidden + low : hidden + low + width],
            right[hidden + low : hidden + low + width],
        ],
        0,
    )
    start = (lax.axis_index("row") * pl.num_programs(0) + step) * rows
    col_valid = cols_ref[lax.axis_index("col")].astype(F32)
    pieces = []
    for i in range(0, rows, 2):
        two = normed[i : i + 2].reshape(2 * cols, pair_width)
        proj = dot(weight, two, NT)
        valid = jnp.concatenate(
            [col_valid * tokens_ref[start + i + n].astype(F32) for n in range(2)], 1
        )
        value = (jnp.tanh(proj[: 2 * width]) + 1.0) * (proj[2 * width :] * valid)
        value = value.astype(BF16)
        pieces += [value[:, :cols], value[:, cols:]]
    value = jnp.swapaxes(jnp.stack(pieces, 0), 0, 1)
    dests, _, share = out_ref.shape[:3]
    for side in range(2):
        part = value[side * width : (side + 1) * width]
        out_ref[:, side] = part.reshape(dests, share, rows, cols)


def first_kernel(
    tokens_ref, cols_ref, pair_ref, left_ref, right_ref, gain_ref, bias_ref, normed_ref, out_ref, *, width
):
    value = pair_ref[...].astype(F32)
    average = jnp.mean(value, axis=-1, keepdims=True)
    centered = value - average
    variance = jnp.mean(centered * centered, axis=-1, keepdims=True)
    normed = (centered * lax.rsqrt(variance + EPS) * gain_ref[...] + bias_ref[...]).astype(BF16)
    normed_ref[...] = normed
    project(normed, pl.program_id(0), tokens_ref, cols_ref, left_ref, right_ref, out_ref, 0, width)


def later_kernel(tokens_ref, cols_ref, normed_ref, left_ref, right_ref, out_ref, *, low, width):
    step = pl.program_id(0)
    project(normed_ref[...], step, tokens_ref, cols_ref, left_ref, right_ref, out_ref, low, width)


def gate_kernel(normed_ref, weight_ref, gate_ref):
    rows, cols, pair_width = normed_ref.shape
    half = jnp.asarray(0.5, BF16)
    proj = dot(normed_ref[...].reshape(rows * cols, pair_width), weight_ref[...] * half)
    gate_ref[...] = (0.5 * jnp.tanh(proj) + 0.5).reshape(gate_ref.shape)


def pick(valid, count):
    size = valid.shape[1]
    above = lax.broadcasted_iota(jnp.int32, (size, size), 0)
    below = lax.broadcasted_iota(jnp.int32, (size, size), 1)
    through = dot(valid, jnp.where(above <= below, 1.0, 0.0).astype(BF16))
    place = jnp.where(valid.astype(F32) > 0.5, through - 1.0, -1.0)[:1]
    order = lax.broadcasted_iota(jnp.int32, (count, size), 0).astype(F32)
    return jnp.where(order == place, 1.0, 0.0)


def picks_kernel(tokens_ref, all_ref, spread_ref, far_ref, near_ref):
    valid = jnp.broadcast_to(tokens_ref[...].astype(F32), (16, tokens_ref.shape[1])).astype(BF16)
    chosen = pick(valid, all_ref.shape[0])
    all_ref[...] = chosen.astype(BF16)
    spread_ref[...] = chosen.T.astype(BF16)
    size = far_ref.shape[1]
    low = pick(valid[:, :size], far_ref.shape[0]).astype(BF16)
    high = pick(valid[:, size:], far_ref.shape[0]).astype(BF16)
    second = lax.axis_index("col") // (lax.axis_size("col") // 2) == 1
    far_ref[...] = jnp.where(second, low, high)
    near_ref[...] = jnp.where(second, high, low)


def panel(ref, side, start, count):
    parts = []
    for z in range(ref.shape[1]):
        block = ref[pl.ds(start, count), z, side, 0]
        parts.append(block.reshape(count * block.shape[1], block.shape[2]))
    return jnp.concatenate(parts, 1)


def own_half():
    return lax.axis_index("col") // (lax.axis_size("col") // 2)


def far_kernel(all_ref, pick_ref, edges_ref, far_ref):
    devices = edges_ref.shape[0]
    left = panel(edges_ref, 0, 0, devices)
    right = panel(edges_ref, 1, (1 - own_half()) * (devices // 2), devices // 2)
    count, size = pick_ref.shape
    main = left.shape[0] * 3 // 4
    left = dot(all_ref[...], left).astype(BF16)
    few = dot(pick_ref[...], right).astype(BF16)
    part = dot(few, left[:main], NT).astype(BF16)
    at = 0
    for n in range(0, main, 128):
        far_ref[0, at : at + count] = part[:, n : n + 128]
        at += count
    rest = left.shape[0] - main
    if rest:
        part = dot(left[main:], right, NT).astype(BF16)
        for n in range(0, size, 128):
            far_ref[0, at : at + rest] = part[:, n : n + 128]
            at += rest


def near_kernel(spread_ref, pick_ref, edges_ref, far_ref, out_ref):
    devices, groups, _, rows, cols = out_ref.shape
    left = panel(edges_ref, 0, 0, devices)
    right = panel(edges_ref, 1, own_half() * (devices // 2), devices // 2)
    total = dot(left, right, NT)
    count, size = pick_ref.shape
    main = left.shape[0] * 3 // 4
    at = main // 128 * count
    part = jnp.concatenate([far_ref[0, n : n + count] for n in range(0, at, count)], 1)
    part = dot(spread_ref[:, :main], part, NT).astype(BF16)
    total = total + dot(part, pick_ref[...])
    rest = spread_ref.shape[1] - main
    if rest:
        ends = range(at, at + size // 128 * rest, rest)
        part = jnp.concatenate([far_ref[0, n : n + rest] for n in ends], 1)
        total = total + dot(spread_ref[:, main:], part)
    total = total.astype(BF16)
    for z in range(groups):
        out_ref[:, z, 0] = total[:, z * cols : (z + 1) * cols].reshape(devices, rows, cols)


def last_kernel(*refs):
    gate_ref, gain_ref, bias_ref, weight_ref = refs[:4]
    out_ref = refs[-1]
    rows, cols = gate_ref.shape[:2]
    hidden = weight_ref.shape[0]
    parts = []
    for ref in refs[4:-1]:
        parts.append(ref[...].reshape(ref.shape[0] * ref.shape[1], rows, cols))
    value = jnp.swapaxes(jnp.concatenate(parts, 0), 0, 1)
    weight = weight_ref[...]
    gain = jnp.broadcast_to(gain_ref[...], (cols, hidden)).T
    bias = jnp.broadcast_to(bias_ref[...], (cols, hidden)).T
    for i in range(rows):
        product = value[i].astype(F32)
        average = jnp.mean(product, axis=0, keepdims=True)
        centered = product - average
        variance = jnp.mean(centered * centered, axis=0, keepdims=True)
        normed = centered * lax.rsqrt(variance + EPS) * gain + bias
        update = dot(normed.astype(BF16), weight, (((0,), (0,)), ((), ())))
        out_ref[i] = (gate_ref[i] * update).astype(BF16)


def shards(
    pair_rep,
    token_mask,
    in_gain,
    in_bias,
    left_weight,
    right_weight,
    gate_weight,
    out_gain,
    out_bias,
    out_weight,
):
    rows, cols, pair_width = pair_rep.shape
    hidden = out_weight.shape[0]
    row_count = lax.axis_size("row")
    col_count = lax.axis_size("col")
    group_cols = col_count // 2
    members = row_count * group_cols
    share = hidden // members
    chunks = CHUNKS if share % CHUNKS == 0 else 1
    share //= chunks
    width = hidden // chunks
    tokens = row_count * rows
    near_tokens = group_cols * cols
    axes = ("row", "col")
    groups = [
        [r * col_count + h * group_cols + z for r in range(row_count) for z in range(group_cols)]
        for h in range(2)
    ]
    across = [(c, (c + group_cols) % col_count) for c in range(col_count)]

    tile = min(ROW_TILE, rows)
    steps = rows // tile
    by_row = lambda *tail: pl.BlockSpec((tile,) + tail, lambda i: (i,) + (0,) * len(tail))
    edge_shape = jax.ShapeDtypeStruct((members, 2, share, rows, cols), BF16)
    edge_spec = pl.BlockSpec((members, 2, share, tile, cols), lambda i: (0, 0, 0, i, 0))
    col_tokens = token_mask.reshape(col_count, 1, cols)
    mask_specs = [pl.BlockSpec(memory_space=pltpu.SMEM), whole(col_tokens)]
    weight_specs = [whole(left_weight), whole(right_weight)]
    edges = []
    normed, first = pl.pallas_call(
        functools.partial(first_kernel, width=width),
        grid=(steps,),
        in_specs=mask_specs
        + [by_row(cols, pair_width)]
        + weight_specs
        + [whole(in_gain[None]), whole(in_bias[None])],
        out_specs=[by_row(cols, pair_width), edge_spec],
        out_shape=[jax.ShapeDtypeStruct(pair_rep.shape, BF16), edge_shape],
        compiler_params=PARAMS,
        name="norm_project",
    )(token_mask, col_tokens, pair_rep, left_weight, right_weight, in_gain[None], in_bias[None])

    def after(value, others):
        return lax.optimization_barrier((value, *others))[0] if others else value

    def exchange(value):
        return lax.all_to_all(value, axes, 0, 0, axis_index_groups=groups, tiled=True)

    def rest_of(sizes, normed, first, token_mask, col_tokens):
        few = near_tokens * sizes[0] // 16
        main = tokens * 3 // 4
        rest = (tokens - main) * sizes[1] // 16
        length = main // 128 * few + near_tokens // 128 * rest
        all_pick, spread, far_pick, near_pick = pl.pallas_call(
            picks_kernel,
            out_shape=[
                jax.ShapeDtypeStruct((main + rest, tokens), BF16),
                jax.ShapeDtypeStruct((tokens, main + rest), BF16),
                jax.ShapeDtypeStruct((few, near_tokens), BF16),
                jax.ShapeDtypeStruct((few, near_tokens), BF16),
            ],
            compiler_params=PARAMS,
            cost_estimate=pl.CostEstimate(
                flops=64 * tokens * tokens, bytes_accessed=6 * tokens * tokens, transcendentals=0
            ),
            name="picks",
        )(token_mask[None])
        edges = [first]
        for t in range(1, chunks):
            edges.append(
                pl.pallas_call(
                    functools.partial(later_kernel, low=t * width, width=width),
                    grid=(steps,),
                    in_specs=mask_specs + [by_row(cols, pair_width)] + weight_specs,
                    out_specs=edge_spec,
                    out_shape=edge_shape,
                    compiler_params=PARAMS,
                    cost_estimate=pl.CostEstimate(
                        flops=4 * rows * cols * pair_width * width * 2,
                        bytes_accessed=3 * rows * cols * pair_width * 2,
                        transcendentals=rows * cols * width * 2,
                    ),
                    name="project",
                )(token_mask, col_tokens, normed, left_weight, right_weight)
            )
        gate = pl.pallas_call(
            gate_kernel,
            grid=(steps,),
            in_specs=[by_row(cols, pair_width), whole(gate_weight)],
            out_specs=by_row(cols, pair_width),
            out_shape=jax.ShapeDtypeStruct(pair_rep.shape, F32),
            compiler_params=PARAMS,
            cost_estimate=pl.CostEstimate(
                flops=2 * rows * cols * pair_width * pair_width,
                bytes_accessed=rows * cols * pair_width * 6,
                transcendentals=rows * cols * pair_width,
            ),
            name="gate",
        )(normed, gate_weight)

        one_h = pl.BlockSpec(
            (row_count, group_cols, 2, 1, rows, cols), lambda h: (0, 0, 0, h, 0, 0)
        )
        far_spec = pl.BlockSpec((1, length, 128), lambda h: (h, 0, 0))
        product_cost = pl.CostEstimate(
            flops=6 * share * tokens * near_tokens * near_tokens,
            bytes_accessed=share * tokens * near_tokens * 6,
            transcendentals=0,
        )
        arrived = []
        sent = []
        fars = []
        for t in range(chunks):
            edge = after(edges[t], arrived[-1:])
            here = exchange(edge).reshape(row_count, group_cols, 2, share, rows, cols)
            arrived.append(here)
            far = pl.pallas_call(
                far_kernel,
                grid=(share,),
                in_specs=[whole(all_pick), whole(far_pick), one_h],
                out_specs=far_spec,
                out_shape=jax.ShapeDtypeStruct((share, length, 128), BF16),
                compiler_params=PARAMS,
                cost_estimate=product_cost,
                name="far_product",
            )(all_pick, far_pick, here)
            sent.append(far)
            fars.append(lax.ppermute(far, "col", across))
        back = []
        totals = []
        for t in range(chunks):
            total = pl.pallas_call(
                near_kernel,
                grid=(share,),
                in_specs=[whole(spread), whole(near_pick), one_h, far_spec],
                out_specs=pl.BlockSpec(
                    (row_count, group_cols, 1, rows, cols), lambda h: (0, 0, h, 0, 0)
                ),
                out_shape=jax.ShapeDtypeStruct((row_count, group_cols, share, rows, cols), BF16),
                compiler_params=PARAMS,
                cost_estimate=product_cost,
                name="near_product",
            )(spread, near_pick, arrived[t], after(fars[t], sent[t + 1 : t + 2] + totals[-1:]))
            totals.append(total)
            back.append(exchange(total.reshape(members, share, rows, cols)))

        piece = pl.BlockSpec((members, share, tile, cols), lambda i: (0, 0, i, 0))
        return pl.pallas_call(
            last_kernel,
            grid=(steps,),
            in_specs=[
                by_row(cols, pair_width),
                whole(out_gain[None]),
                whole(out_bias[None]),
                whole(out_weight),
            ]
            + [piece] * chunks,
            out_specs=by_row(cols, pair_width),
            out_shape=jax.ShapeDtypeStruct(pair_rep.shape, BF16),
            compiler_params=PARAMS,
            name="norm_out",
        )(gate, out_gain[None], out_bias[None], out_weight, *back)

    count = jnp.sum(token_mask.reshape(2, near_tokens), axis=1)
    most, over = jnp.max(count), jnp.sum(count) - tokens * 3 // 4
    fits = [
        (most <= near_tokens * few // 16) & (over <= tokens // 4 * rest // 16)
        for few, rest in SIZES[:-1]
    ]
    number = len(SIZES) - 1
    for n in range(len(SIZES) - 2, -1, -1):
        number = jnp.where(fits[n], n, number)
    branches = [functools.partial(rest_of, sizes) for sizes in SIZES]
    return lax.switch(number, branches, normed, first, token_mask, col_tokens)


def solution(mesh):
    placed = (P("row", "col", None), P(), P(), P(), P(), P(), P(), P(), P(), P())
    return jax.shard_map(
        shards, mesh=mesh, in_specs=placed, out_specs=P("row", "col", None), check_vma=False
    )
```

time: 198 us -> 167 us (0.84)
  waiting for transfers between devices: 126 us -> 92.7 us
  local copies, waits for them, and re-layouts: 6.37 us -> 3.77 us
  between operations: 0.09 us -> 2.62 us
    ppermute x2, waiting for transfers between devices: 92.9 us -> 27.1 us  [rest_of(): fars.append(lax.ppermute(far, 'col', across))]
    all_to_all x4, waiting for transfers between devices: 32.8 us -> 65.6 us  [exchange(): lax.all_to_all(value, axes, 0, 0, axis_index_groups=groups, tiled=True)]
    unnamed x16, local copies, waits for them, and re-layouts: 3.33 us -> 1.34 us
    pallas_call x8 -> x9, Pallas kernels: 39.7 us -> 40.6 us  [the longest x2 10.6 us: rest_of(): pl.pallas_call(near_kernel, grid=(share,), in_specs=[whole(spread), whole...]
  transfers between devices with their start and end apart: 6 -> 6, of which waited for: 4 -> 4; matrix products, arithmetic and copies ran while one was open for 0% -> 0% of each run, Pallas kernels for 13% -> 14%
where the time goes in v2:
time: 167 us; the launch traced here: 166 us
  waiting for transfers between devices  92.7 us (56%)
  Pallas kernels  40.6 us (24%)
  starting transfers between devices  23.6 us (14%)
  local copies, waits for them, and re-layouts  3.77 us (2%)
  between operations  2.62 us (2%)
  other arithmetic  2.08 us (1%)
    all_to_all x4, waiting for transfers between devices, exchange(): lax.all_to_all(value, axes, 0, 0, axis_index_groups=groups, tiled=True)  65.6 us
    ppermute x2, waiting for transfers between devices, rest_of(): fars.append(lax.ppermute(far, 'col', across))  27.1 us
    all_to_all x4, starting transfers between devices, exchange(): lax.all_to_all(value, axes, 0, 0, axis_index_groups=groups, tiled=True)  18.8 us
    pallas_call x2, Pallas kernels, rest_of(): pl.pallas_call(near_kernel, grid=(share,), in_specs=[whole(spread), whole...  10.6 us
    pallas_call x2, Pallas kernels, rest_of(): pl.pallas_call(far_kernel, grid=(share,), in_specs=[whole(all_pick), whol...  9.29 us
    pallas_call x1, Pallas kernels, shards(): pl.pallas_call(functools.partial(first_kernel, width=width), grid=(steps,...  7.03 us
    pallas_call x1, Pallas kernels, rest_of(): pl.pallas_call(last_kernel, grid=(steps,), in_specs=[by_row(cols, pair_wi...  5.27 us
    ppermute x2, starting transfers between devices, rest_of(): fars.append(lax.ppermute(far, 'col', across))  4.83 us
  transfers between devices with their start and end apart: 6, of which 4 were waited for; matrix products, arithmetic and copies ran while one was open for 0% of the time, Pallas kernels for 14%

profile of v2, /device:TPU:0, one launch (start us, length us, event | category | flops | bytes accessed | tf_op | source)
XLA Modules:
  0.0 165.8 jit_solution(544254768906880861)
XLA Ops:
  2.2 1.3 reduce_sum.19
  5.4 7.0 %norm_project.1 = (bf16[64,128,128]{2,1,0:T(8,128)(2,1)S(1)}, bf16[16,2,4,64,128]{4,3,2,1,0:T(8,128)(2,1)}) custom-call(s32[512]{0:T(512)} %tokens_ref.1, s32[4,1,128]{2,1,0:T(1,128)} %bitcast.39, bf16[64,128,128]{2,1,0:T(8,128)(2,1)} %pair_ref.1, bf16[128,256]{1,0:T(8,128)(2,1)} %left_ref.1, bf16[128,256]{1,0:T(8,128)(2,1)} %right_ref.1, ...), custom_call_target="tpu_custom_call" | custom-call | tf_op jit(solution)/shard_map/norm_project/pallas_call | solution.py:225
  12.5 151.9 %conditional.1 = (bf16[64,128,128]{2,1,0:T(8,128)(2,1)S(1)}) conditional(s32[]{:T(128)} %clamp.3, (bf16[64,128,128]{2,1,0:T(8,128)(2,1)S(1)}, bf16[128,128]{1,0:T(8,128)(2,1)S(1)}, f32[128]{0:T(128)S(1)}, f32[128]{0:T(128)S(1)}, s32[512]{0:T(512)S(1)}, /*index=5*/bf16[16,2,4,64,128]{4,3,2,1,0:T(8,128)(2,1)}, ...), branch_computations={%region_3.4_spmd, %region_4.5_spmd, %region_5.6_spmd, %region_6.7_... | conditional | flops 4043309056 | bytes 66584876 | solution.py:369
  12.5 6.4 %all-to-all-start = ((bf16[16,2,4,64,128]{4,3,2,1,0:T(8,128)(2,1)}), bf16[16,2,4,64,128]{4,3,2,1,0:T(8,128)(2,1)}, u32[]{:S(2)}, u32[]{:S(2)}) async-start(bf16[16,2,4,64,128]{4,3,2,1,0:T(8,128)(2,1)} %get-tuple-element.98), calls=%async_computation | async-start | bytes 4194304 | tf_op jit(solution)/shard_map/cond/branch_0_fun/all_to_all | solution.py:242
  18.9 4.2 %project.4 = bf16[16,2,4,64,128]{4,3,2,1,0:T(8,128)(2,1)} custom-call(s32[512]{0:T(512)S(1)} %bitcast.44, s32[4,1,128]{2,1,0:T(1,128)S(1)} %get-tuple-element.101.cols_ref, bf16[64,128,128]{2,1,0:T(8,128)(2,1)S(1)} %get-tuple-element.88.normed_ref, bf16[128,256]{1,0:T(8,128)(2,1)S(1)} %get-tuple-element.102.left_ref, ...), custom_call_target="tpu_custom_call" | custom-call | flops 536870912 | bytes 6291456 | tf_op jit(solution)/shard_map/cond/branch_0_fun/project/pallas_call | solution.py:266
  23.1 23.5 %all-to-all-done = bf16[16,2,4,64,128]{4,3,2,1,0:T(8,128)(2,1)} async-done(((bf16[16,2,4,64,128]{4,3,2,1,0:T(8,128)(2,1)}), bf16[16,2,4,64,128]{4,3,2,1,0:T(8,128)(2,1)}, u32[]{:S(2)}, u32[]{:S(2)}) %all-to-all-start) | async-done | bytes 2097184 | tf_op jit(solution)/shard_map/cond/branch_0_fun/all_to_all | solution.py:242
  46.6 4.5 %all-to-all-start.1 = ((bf16[16,2,4,64,128]{4,3,2,1,0:T(8,128)(2,1)}), bf16[16,2,4,64,128]{4,3,2,1,0:T(8,128)(2,1)}, u32[]{:S(2)}, u32[]{:S(2)}) async-start(bf16[16,2,4,64,128]{4,3,2,1,0:T(8,128)(2,1)} %project.4), calls=%async_computation.1 | async-start | bytes 4194304 | tf_op jit(solution)/shard_map/cond/branch_0_fun/all_to_all | solution.py:242
  51.1 1.3 picks.4
  52.4 4.6 %far_product.8 = bf16[4,576,128]{2,1,0:T(8,128)(2,1)} custom-call(bf16[384,512]{1,0:T(8,128)(2,1)} %get-tuple-element.99.all_ref, bf16[192,256]{1,0:T(8,128)(2,1)} %get-tuple-element.100.pick_ref, bf16[8,2,2,4,64,128]{5,4,3,2,1,0:T(8,128)(2,1)} %bitcast.3.edges_ref), custom_call_target="tpu_custom_call" | custom-call | flops 805306368 | bytes 3145728 | tf_op jit(solution)/shard_map/cond/branch_0_fun/far_product/pallas_call | solution.py:312
  57.0 2.6 %collective-permute-start = (bf16[4,576,128]{2,1,0:T(8,128)(2,1)}, bf16[4,576,128]{2,1,0:T(8,128)(2,1)S(1)}, u32[]{:S(2)}, u32[]{:S(2)}) collective-permute-start(bf16[4,576,128]{2,1,0:T(8,128)(2,1)} %far_product.8), channel_id=1, source_target_pairs={{0,2},{1,3},{2,0},{3,1},{4,6},{5,7},{6,4},{7,5},{8,10},{9,11},{10,... | collective-permute-start | bytes 1769480 | tf_op jit(solution)/shard_map/cond/branch_0_fun/ppermute | solution.py:323
  59.6 30.1 %all-to-all-done.1 = bf16[16,2,4,64,128]{4,3,2,1,0:T(8,128)(2,1)} async-done(((bf16[16,2,4,64,128]{4,3,2,1,0:T(8,128)(2,1)}), bf16[16,2,4,64,128]{4,3,2,1,0:T(8,128)(2,1)}, u32[]{:S(2)}, u32[]{:S(2)}) %all-to-all-start.1) | async-done | bytes 2097184 | tf_op jit(solution)/shard_map/cond/branch_0_fun/all_to_all | solution.py:242
  89.7 4.6 %far_product.9 = bf16[4,576,128]{2,1,0:T(8,128)(2,1)} custom-call(bf16[384,512]{1,0:T(8,128)(2,1)} %get-tuple-element.99.all_ref, bf16[192,256]{1,0:T(8,128)(2,1)} %get-tuple-element.100.pick_ref, bf16[8,2,2,4,64,128]{5,4,3,2,1,0:T(8,128)(2,1)} %bitcast.4.edges_ref), custom_call_target="tpu_custom_call" | custom-call | flops 805306368 | bytes 3145728 | tf_op jit(solution)/shard_map/cond/branch_0_fun/far_product/pallas_call | solution.py:312
  94.4 0.8 copy-done.13
  95.2 5.3 %near_product.8 = bf16[8,2,4,64,128]{4,3,2,1,0:T(8,128)(2,1)} custom-call(bf16[512,384]{1,0:T(8,128)(2,1)} %get-tuple-element.96.spread_ref, bf16[192,256]{1,0:T(8,128)(2,1)} %get-tuple-element.97.pick_ref, bf16[8,2,2,4,64,128]{5,4,3,2,1,0:T(8,128)(2,1)} %bitcast.3.edges_ref, bf16[4,576,128]{2,1,0:T(8,128)(2,1)} %copy-done.13), custom_call_target="tpu_custom_call" | custom-call | flops 805306368 | bytes 3145728 | tf_op jit(solution)/shard_map/cond/branch_0_fun/near_product/pallas_call | solution.py:327
  100.5 3.7 %all-to-all-start.2 = ((bf16[16,4,64,128]{3,2,1,0:T(8,128)(2,1)}), bf16[16,4,64,128]{3,2,1,0:T(8,128)(2,1)S(1)}, u32[]{:S(2)}, u32[]{:S(2)}) async-start(bf16[16,4,64,128]{3,2,1,0:T(8,128)(2,1)} %bitcast.35), calls=%async_computation.2 | async-start | bytes 2097152 | tf_op jit(solution)/shard_map/cond/branch_0_fun/all_to_all | solution.py:242
  104.1 2.2 %collective-permute-start.1 = (bf16[4,576,128]{2,1,0:T(8,128)(2,1)}, bf16[4,576,128]{2,1,0:T(8,128)(2,1)S(1)}, u32[]{:S(2)}, u32[]{:S(2)}) collective-permute-start(bf16[4,576,128]{2,1,0:T(8,128)(2,1)} %far_product.9), channel_id=1, source_target_pairs={{0,2},{1,3},{2,0},{3,1},{4,6},{5,7},{6,4},{7,5},{8,10},{9,11},{10,... | collective-permute-start | bytes 1769480 | tf_op jit(solution)/shard_map/cond/branch_0_fun/ppermute | solution.py:323
  106.4 27.1 %collective-permute-done.1.far_ref = bf16[4,576,128]{2,1,0:T(8,128)(2,1)S(1)} collective-permute-done((bf16[4,576,128]{2,1,0:T(8,128)(2,1)}, bf16[4,576,128]{2,1,0:T(8,128)(2,1)S(1)}, u32[]{:S(2)}, u32[]{:S(2)}) %collective-permute-start.1) | collective-permute-done | bytes 589856 | tf_op jit(solution)/shard_map/cond/branch_0_fun/ppermute | solution.py:323
  133.5 0.8 copy-done.14
  134.3 5.3 %near_product.9 = bf16[8,2,4,64,128]{4,3,2,1,0:T(8,128)(2,1)} custom-call(bf16[512,384]{1,0:T(8,128)(2,1)} %get-tuple-element.96.spread_ref, bf16[192,256]{1,0:T(8,128)(2,1)} %get-tuple-element.97.pick_ref, bf16[8,2,2,4,64,128]{5,4,3,2,1,0:T(8,128)(2,1)} %bitcast.4.edges_ref, bf16[4,576,128]{2,1,0:T(8,128)(2,1)} %copy-done.14), custom_call_target="tpu_custom_call" | custom-call | flops 805306368 | bytes 3145728 | tf_op jit(solution)/shard_map/cond/branch_0_fun/near_product/pallas_call | solution.py:327
  139.6 4.3 %all-to-all-start.3 = ((bf16[16,4,64,128]{3,2,1,0:T(8,128)(2,1)}), bf16[16,4,64,128]{3,2,1,0:T(8,128)(2,1)}, u32[]{:S(2)}, u32[]{:S(2)}) async-start(bf16[16,4,64,128]{3,2,1,0:T(8,128)(2,1)} %bitcast.37), calls=%async_computation.3 | async-start | bytes 2097152 | tf_op jit(solution)/shard_map/cond/branch_0_fun/all_to_all | solution.py:242
  143.9 3.0 %gate.4.refs_0_ = f32[64,128,128]{2,1,0:T(8,128)} custom-call(bf16[64,128,128]{2,1,0:T(8,128)(2,1)S(1)} %get-tuple-element.88.normed_ref, bf16[128,128]{1,0:T(8,128)(2,1)S(1)} %get-tuple-element.90.weight_ref), custom_call_target="tpu_custom_call" | custom-call | flops 268435456 | bytes 6291456 | tf_op jit(solution)/shard_map/cond/branch_0_fun/gate/pallas_call | solution.py:281
  146.9 12.0 %all-to-all-done.3.refs_5_ = bf16[16,4,64,128]{3,2,1,0:T(8,128)(2,1)} async-done(((bf16[16,4,64,128]{3,2,1,0:T(8,128)(2,1)}), bf16[16,4,64,128]{3,2,1,0:T(8,128)(2,1)}, u32[]{:S(2)}, u32[]{:S(2)}) %all-to-all-start.3) | async-done | bytes 1048608 | tf_op jit(solution)/shard_map/cond/branch_0_fun/all_to_all | solution.py:242
  158.9 5.3 %norm_out.4 = bf16[64,128,128]{2,1,0:T(8,128)(2,1)S(1)} custom-call(f32[64,128,128]{2,1,0:T(8,128)} %gate.4.refs_0_, f32[1,128]{1,0:T(1,128)S(1)} %bitcast.52, f32[1,128]{1,0:T(1,128)S(1)} %bitcast.56, bf16[128,128]{1,0:T(8,128)(2,1)S(1)} %get-tuple-element.94.refs_3_, bf16[16,4,64,128]{3,2,1,0:T(8,128)(2,1)} %copy-done, ...), custom_call_target="tpu_custom_call" | custom-call | tf_op jit(solution)/shard_map/cond/branch_0_fun/norm_out/pallas_call | solution.py:343
  164.5 1.3 copy-done.4
  (24 shorter events, 1.6 us)
Async XLA Ops:
  0.0 12.5 %copy-start.17 = (s32[512]{0:T(512)S(1)}, s32[512]{0:T(512)}, u32[]{:S(2)}) copy-start(s32[512]{0:T(512)} %tokens_ref.1) | copy-start | bytes 6148
  0.0 12.5 %copy-start.5 = (bf16[128,256]{1,0:T(8,128)(2,1)S(1)}, bf16[128,256]{1,0:T(8,128)(2,1)}, u32[]{:S(2)}) copy-start(bf16[128,256]{1,0:T(8,128)(2,1)} %left_ref.1) | copy-start | bytes 196612
  0.0 12.5 %copy-start.6 = (bf16[128,256]{1,0:T(8,128)(2,1)S(1)}, bf16[128,256]{1,0:T(8,128)(2,1)}, u32[]{:S(2)}) copy-start(bf16[128,256]{1,0:T(8,128)(2,1)} %right_ref.1) | copy-start | bytes 196612
  0.0 12.5 %copy-start.15 = (bf16[128,128]{1,0:T(8,128)(2,1)S(1)}, bf16[128,128]{1,0:T(8,128)(2,1)}, u32[]{:S(2)}) copy-start(bf16[128,128]{1,0:T(8,128)(2,1)} %param.20) | copy-start | bytes 98308
  0.0 12.5 %copy-start.18 = (f32[128]{0:T(128)S(1)}, f32[128]{0:T(128)}, u32[]{:S(2)}) copy-start(f32[128]{0:T(128)} %param.21) | copy-start | bytes 1540
  0.0 12.5 %copy-start.19 = (f32[128]{0:T(128)S(1)}, f32[128]{0:T(128)}, u32[]{:S(2)}) copy-start(f32[128]{0:T(128)} %param.22) | copy-start | bytes 1540
  0.0 12.5 %copy-start.16 = (bf16[128,128]{1,0:T(8,128)(2,1)S(1)}, bf16[128,128]{1,0:T(8,128)(2,1)}, u32[]{:S(2)}) copy-start(bf16[128,128]{1,0:T(8,128)(2,1)} %param.23) | copy-start | bytes 98308
  12.5 34.1 %all-to-all-start = ((bf16[16,2,4,64,128]{4,3,2,1,0:T(8,128)(2,1)}), bf16[16,2,4,64,128]{4,3,2,1,0:T(8,128)(2,1)}, u32[]{:S(2)}, u32[]{:S(2)}) async-start(bf16[16,2,4,64,128]{4,3,2,1,0:T(8,128)(2,1)} %get-tuple-element.98), calls=%async_computation | async-start | bytes 4194304 | tf_op jit(solution)/shard_map/cond/branch_0_fun/all_to_all | solution.py:242
  46.6 43.1 %all-to-all-start.1 = ((bf16[16,2,4,64,128]{4,3,2,1,0:T(8,128)(2,1)}), bf16[16,2,4,64,128]{4,3,2,1,0:T(8,128)(2,1)}, u32[]{:S(2)}, u32[]{:S(2)}) async-start(bf16[16,2,4,64,128]{4,3,2,1,0:T(8,128)(2,1)} %project.4), calls=%async_computation.1 | async-start | bytes 4194304 | tf_op jit(solution)/shard_map/cond/branch_0_fun/all_to_all | solution.py:242
  57.0 37.4 %collective-permute-start = (bf16[4,576,128]{2,1,0:T(8,128)(2,1)}, bf16[4,576,128]{2,1,0:T(8,128)(2,1)S(1)}, u32[]{:S(2)}, u32[]{:S(2)}) collective-permute-start(bf16[4,576,128]{2,1,0:T(8,128)(2,1)} %far_product.8), channel_id=1, source_target_pairs={{0,2},{1,3},{2,0},{3,1},{4,6},{5,7},{6,4},{7,5},{8,10},{9,11},{10,... | collective-permute-start | bytes 1769480 | tf_op jit(solution)/shard_map/cond/branch_0_fun/ppermute | solution.py:323
  94.4 0.8 copy-start.13
  100.5 39.1 %all-to-all-start.2 = ((bf16[16,4,64,128]{3,2,1,0:T(8,128)(2,1)}), bf16[16,4,64,128]{3,2,1,0:T(8,128)(2,1)S(1)}, u32[]{:S(2)}, u32[]{:S(2)}) async-start(bf16[16,4,64,128]{3,2,1,0:T(8,128)(2,1)} %bitcast.35), calls=%async_computation.2 | async-start | bytes 2097152 | tf_op jit(solution)/shard_map/cond/branch_0_fun/all_to_all | solution.py:242
  104.1 29.3 %collective-permute-start.1 = (bf16[4,576,128]{2,1,0:T(8,128)(2,1)}, bf16[4,576,128]{2,1,0:T(8,128)(2,1)S(1)}, u32[]{:S(2)}, u32[]{:S(2)}) collective-permute-start(bf16[4,576,128]{2,1,0:T(8,128)(2,1)} %far_product.9), channel_id=1, source_target_pairs={{0,2},{1,3},{2,0},{3,1},{4,6},{5,7},{6,4},{7,5},{8,10},{9,11},{10,... | collective-permute-start | bytes 1769480 | tf_op jit(solution)/shard_map/cond/branch_0_fun/ppermute | solution.py:323
  133.5 0.8 copy-start.14
  139.6 7.3 %copy-start = (bf16[16,4,64,128]{3,2,1,0:T(8,128)(2,1)}, bf16[16,4,64,128]{3,2,1,0:T(8,128)(2,1)S(1)}, u32[]{:S(2)}) copy-start(bf16[16,4,64,128]{3,2,1,0:T(8,128)(2,1)S(1)} %all-to-all-done.2.refs_4_) | copy-start | bytes 3145732 | tf_op jit(solution)/shard_map/cond
  139.6 19.3 %all-to-all-start.3 = ((bf16[16,4,64,128]{3,2,1,0:T(8,128)(2,1)}), bf16[16,4,64,128]{3,2,1,0:T(8,128)(2,1)}, u32[]{:S(2)}, u32[]{:S(2)}) async-start(bf16[16,4,64,128]{3,2,1,0:T(8,128)(2,1)} %bitcast.37), calls=%async_computation.3 | async-start | bytes 2097152 | tf_op jit(solution)/shard_map/cond/branch_0_fun/all_to_all | solution.py:242
  164.4 1.3 copy-start.4
